TPU v7x, 32 devices: a whole 2x2x4 slice. The times are simulated.
32 devices in a mesh: head: 4 (over z), page: 8 (over y, x, core).
Axes of the slice: x: 2, y: 2, z: 4, core: 2. Of those that a mesh axis runs over, the one named last changes fastest.
Arguments:
- doc_states: bfloat16 [512, 2048], P('page'), may hold values from -6 to 6
- gain_attn: float32 [2048], replicated, may hold values from 0.1 to 1.9
- query_weight: bfloat16 [2048, 2048], P(None, 'head'), may hold values from -0.125 to 0.125
- cache_keys: bfloat16 [16, 128, 2048], P('page', None, 'head'), may hold values from -144 to 144
- cache_values: bfloat16 [16, 128, 2048], P('page', None, 'head'), may hold values from -6 to 6
- rel_bucket: int32 [16, 128], P('page'), may hold values from 0 to 31
- bias_table: float32 [32, 32], P(None, 'head'), may hold values from -4 to 4
- out_weight: bfloat16 [2048, 2048], P('head'), may hold values from -0.125 to 0.125
- gain_ffn: float32 [2048], replicated, may hold values from 0.1 to 1.9
- wi_gate: bfloat16 [2048, 5120], P(None, 'head'), may hold values from -0.125 to 0.125
- wi_up: bfloat16 [2048, 5120], P(None, 'head'), may hold values from -0.125 to 0.125
- wo_ffn: bfloat16 [5120, 2048], P('head'), may hold values from -0.078125 to 0.078125
- score_vector: float32 [2048], replicated, may hold values from -0.125 to 0.125
- query_lengths: int32 [8], replicated, may hold values from 1 to 256
- doc_query: int32 [64], replicated, may hold values from 0 to 7
- doc_of_token: int32 [512], replicated, may hold values from 0 to 63, as said below
- page_table: int32 [16], replicated, may hold values from 0 to 15, each once
Outputs:
- doc_scores: float32 [64], P('page')
Inputs may be any that keep to these rules, and one draw needn't show every extreme that they name: page_table lists every physical page once. `doc_of_token`: the tokens of each document form one contiguous run of 1 to 256 tokens; every document has one run, and some document has exactly 256 tokens.
All inputs are finite; a program needn't handle non-finite values.
Results may differ from a plain program's by a relative error of at most 0.03.
Values may be sent and summed in bfloat16 or wider, within the bound.
A program may use at most 320 MiB of HBM per device.

v0:
```python
import functools

import jax
import jax.numpy as jnp
from jax import lax
from jax.experimental import pallas as pl
from jax.experimental.pallas import tpu as pltpu
from jax.sharding import PartitionSpec as P

NQ = 8
FAR = -1e30
MESH = pl.DeviceIdType.MESH
F32 = jnp.float32
BF16 = jnp.bfloat16


def iota(shape, dim):
    return lax.broadcasted_iota(jnp.int32, shape, dim)


def dot(a, b):
    return jnp.dot(a, b, preferred_element_type=F32)


def dot_last(a, b):
    return lax.dot_general(a, b, (((1,), (1,)), ((), ())), preferred_element_type=F32)


def three_parts(value):
    first = value.astype(BF16).astype(F32)
    second = (value - first).astype(BF16).astype(F32)
    third = (value - first - second).astype(BF16).astype(F32)
    return first, second, third


def kernel(
    nz, npg,
    doc_hbm, ga_hbm, qw_hbm, ck_hbm, cv_hbm, rb_hbm, bt_hbm, ow_hbm, gf_hbm, wg_hbm, wu_hbm,
    wo_hbm, sv_hbm, ql_hbm, dq_hbm, dtok_hbm, pt_hbm,
    out,
    ga, rb, bt, gf, sv, ql, dq, dtok, pt,
    doc, qw, kbuf, vbuf, rbx, ow, wg, wu, wo, kz, vz, kbias, tokq_row, keyq_row,
    q_all, ax_out, ax, rs_out, rs, ag, fz, fp, w2,
    lsem, pair_s, pair_r, q_s, q_r, a_s, a_r, r_s, r_r, g_s, g_r, z_s, z_r, p_s, p_r,
):
    nc = npg // 2
    z = lax.axis_index("head")
    p = lax.axis_index("page")
    core = p % 2
    chip = p // 2
    partner = p + 1 - 2 * core
    toks, model = doc.shape
    width = qw.shape[1]
    heads = bt.shape[0]
    depth = width // heads
    pages, page_len = rb.shape
    span = 2 * pages * page_len
    total_toks = dtok.shape[1]
    ndoc = dq.shape[0]
    doc_dev = ndoc // npg
    block = model // nz
    all_pages = pt.shape[0]
    max_pages = all_pages // NQ

    barrier = pltpu.get_barrier_semaphore()
    for k in range(1, npg):
        pl.semaphore_signal(barrier, inc=1, device_id=(z, (p + k) % npg), device_id_type=MESH)
    for k in range(1, nz):
        pl.semaphore_signal(barrier, inc=1, device_id=((z + k) % nz, p), device_id_type=MESH)

    moves = []
    for n, (src, dst) in enumerate([
        (doc_hbm, doc), (ga_hbm, ga), (qw_hbm, qw),
        (ck_hbm, kbuf.at[0]), (cv_hbm, vbuf.at[0]),
        (ow_hbm, ow), (wo_hbm, wo), (wg_hbm, wg), (wu_hbm, wu),
        (rb_hbm, rb), (bt_hbm, bt), (gf_hbm, gf), (sv_hbm, sv),
        (ql_hbm, ql), (dq_hbm, dq), (dtok_hbm, dtok), (pt_hbm, pt),
    ]):
        moves.append(pltpu.make_async_copy(src, dst, lsem.at[n]))
    doc_in, ga_in, qw_in, k_in, v_in, ow_in, wo_in, wg_in, wu_in = moves[:9]
    small_in = moves[9:]
    for move in [doc_in, ga_in, qw_in] + small_in + [k_in, v_in]:
        move.start()

    pl.semaphore_wait(barrier, npg - 1 + nz - 1)
    pairs = []
    for n, (src, dst) in enumerate([(ck_hbm, kbuf.at[1]), (cv_hbm, vbuf.at[1]), (rb_hbm, rbx)]):
        copy = pltpu.make_async_remote_copy(
            src_ref=src, dst_ref=dst, send_sem=pair_s.at[n], recv_sem=pair_r.at[n],
            device_id=(z, partner), device_id_type=MESH,
        )
        copy.start()
        pairs.append(copy)

    doc_in.wait()
    ga_in.wait()
    x = doc[...].astype(F32)
    scale = lax.rsqrt(jnp.mean(x * x, axis=1, keepdims=True) + 1e-6)
    normed = (x * scale * ga[...]).astype(BF16)
    qw_in.wait()
    q_all[0] = dot(normed, qw[...]).astype(BF16)

    def query_copy(k):
        return pltpu.make_async_remote_copy(
            src_ref=q_all.at[0], dst_ref=q_all.at[k], send_sem=q_s.at[k], recv_sem=q_r.at[k],
            device_id=(z, ((chip + k) % nc) * 2 + core), device_id_type=MESH,
        )

    for k in range(1, nc):
        query_copy(k).start()
    for move in (ow_in, wo_in, wg_in, wu_in):
        move.start()
    for move in small_in:
        move.wait()

    docs = dtok[...]

    def fill(step, carry):
        for j in range(16):
            d = step * 16 + j
            carry = jnp.where(docs == d, dq[d], carry)
        return carry

    tokq_row[...] = lax.fori_loop(
        0, ndoc // 16, fill, jnp.zeros((1, total_toks), jnp.int32)
    ).astype(F32)
    lane = iota((1, span), 1)
    half = span // 2
    page = jnp.where(lane < half, p * pages + lane // page_len, partner * pages + (lane - half) // page_len)
    owner = jnp.full((1, span), -1.0, F32)
    left = jnp.zeros((1, span), jnp.int32)
    for s in range(all_pages):
        hit = page == pt[s]
        owner = jnp.where(hit, float(s // max_pages), owner)
        left = jnp.where(hit, ql[s // max_pages] - (s % max_pages) * page_len, left)
    keyq_row[...] = jnp.where(lane % page_len < left, owner, -1.0)

    side = iota((1, 128), 1) // depth
    side_mask = [(side == s).astype(F32).astype(BF16) for s in range(128 // depth)]
    per = 128 // depth

    def split_heads(buf, dest, slot):
        for j in range(pages):
            rows = pl.ds((slot * pages + j) * page_len, page_len)
            for h in range(heads):
                g = h // per
                dest[h, rows, :] = buf[slot, j, :, g * 128:(g + 1) * 128] * side_mask[h % per]

    buckets = bt.shape[1]

    def bias_of(ref, slot):
        for j in range(pages):
            onehot = (ref[j:j + 1, :] == iota((buckets, page_len), 0)).astype(F32)
            part = lax.dot_general(
                bt[...], onehot, (((1,), (0,)), ((), ())),
                precision=lax.Precision.HIGHEST, preferred_element_type=F32,
            )
            at = (slot * pages + j) * page_len
            kbias[:, at:at + page_len] = part

    bias_of(rb, 0)
    k_in.wait()
    split_heads(kbuf, kz, 0)
    v_in.wait()
    split_heads(vbuf, vz, 0)
    for copy in pairs:
        copy.wait_recv()
    bias_of(rbx, 1)
    split_heads(kbuf, kz, 1)
    split_heads(vbuf, vz, 1)

    spot = iota((1, 128), 1)

    def token_column(row, first):
        hit = iota((toks, total_toks), 1) == iota((toks, total_toks), 0) + first
        return jnp.sum(jnp.where(hit, row, 0.0), axis=1, keepdims=True)

    def attend(k, dest):
        source = ((chip - k + nc) % nc) * 2 + core
        column = token_column(tokq_row[...], source * toks)
        far = jnp.where(column == keyq_row[...], 0.0, FAR)
        stats = jnp.zeros((toks, 128), F32)
        for base in range(0, heads, 4):
            some = range(base, base + 4)
            scores = [
                dot_last(q_all[k, :, h // per * 128:(h // per + 1) * 128], kz[h])
                + (far + kbias[h:h + 1, :])
                for h in some
            ]
            tops = [jnp.max(score, axis=1, keepdims=True) for score in scores]
            weights = [jnp.exp(score - top) for score, top in zip(scores, tops)]
            totals = [jnp.sum(weight, axis=1, keepdims=True) for weight in weights]
            parts = [dot(weight.astype(BF16), vz[h]) for weight, h in zip(weights, some)]
            for h, top, total in zip(some, tops, totals):
                mine = spot % heads == h
                stats = jnp.where(mine & (spot < 3 * heads), top, stats)
                stats = jnp.where(mine & (spot >= 3 * heads), total, stats)
            for j in range(0, 4, per):
                g = (base + j) // per
                dest[:, g * 128:(g + 1) * 128] = sum(parts[j:j + per]).astype(BF16)
        a, b, c = three_parts(stats)
        part = (spot // heads) % 3
        packed = jnp.where(part == 0, a, jnp.where(part == 1, b, c))
        dest[:, width:] = jnp.where(spot < 6 * heads, packed, 0.0).astype(BF16)

    def partial_copy(k):
        return pltpu.make_async_remote_copy(
            src_ref=ax_out.at[k], dst_ref=ax.at[k], send_sem=a_s.at[k], recv_sem=a_r.at[k],
            device_id=(z, ((chip - k + nc) % nc) * 2 + core), device_id_type=MESH,
        )

    attend(0, ax.at[0])

    def serve(k, carry):
        query_copy(k).wait_recv()
        attend(k, ax_out.at[k])
        partial_copy(k).start()
        return carry

    lax.fori_loop(1, nc, serve, 0)

    wo_in.wait()
    a, b, c = three_parts(sv[...])
    line = iota((16, model), 0)
    folded = jnp.where(line == 0, a, jnp.where(line == 1, b, jnp.where(line == 2, c, 0.0)))
    w2[...] = jnp.sum(dot_last(folded.astype(BF16), wo[...]), axis=0, keepdims=True)
    own_docs = token_column(docs.astype(F32), p * toks)
    fin = fz.shape[2]
    member = (own_docs == iota((toks, fin), 1).astype(F32)).astype(F32)
    mine = p * doc_dev + iota((doc_dev, total_toks), 0)
    counts = jnp.sum((docs == mine).astype(F32), axis=1, keepdims=True)
    ow_in.wait()

    lanes = iota((128, width), 0)
    same = lanes % heads == iota((128, width), 1) // depth
    pick_top = (same & (lanes < 3 * heads)).astype(F32).astype(BF16)
    pick_total = (same & (lanes >= 3 * heads) & (lanes < 6 * heads)).astype(F32).astype(BF16)
    for k in range(1, nc):
        partial_copy(k).wait_recv()
    best = dot(ax[0, :, width:], pick_top)
    for k in range(1, nc):
        best = jnp.maximum(best, dot(ax[k, :, width:], pick_top))
    total = jnp.zeros((toks, width), F32)
    sums = jnp.zeros((toks, width), F32)
    for k in range(nc):
        stat = ax[k, :, width:]
        factor = jnp.exp(dot(stat, pick_top) - best)
        total += factor * dot(stat, pick_total)
        sums += factor * ax[k, :, :width].astype(F32)
    context = (sums / total).astype(BF16)

    def block_of(k):
        return pl.ds(pl.multiple_of(((z + k) % nz) * block, block), block)

    def scatter_copy(k):
        return pltpu.make_async_remote_copy(
            src_ref=rs_out.at[k], dst_ref=rs.at[k], send_sem=r_s.at[k], recv_sem=r_r.at[k],
            device_id=((z + k) % nz, p), device_id_type=MESH,
        )

    order = sorted(range(1, nz), key=lambda k: -min(k, nz - k))
    for k in order:
        rs_out[k] = dot(context, ow[:, block_of(k)]).astype(BF16)
        scatter_copy(k).start()
    hidden = doc[:, block_of(0)].astype(F32) + dot(context, ow[:, block_of(0)])
    for k in reversed(order):
        scatter_copy(k).wait_recv()
        hidden += rs[k].astype(F32)

    def gather_copy(k):
        return pltpu.make_async_remote_copy(
            src_ref=ag.at[0], dst_ref=ag.at[k], send_sem=g_s.at[k], recv_sem=g_r.at[k],
            device_id=((z + k) % nz, p), device_id_type=MESH,
        )

    gain = gf[:, block_of(0)]
    ag[0] = (hidden * gain).astype(BF16)
    for k in order:
        gather_copy(k).start()
    tok_score = jnp.sum(hidden * sv[:, block_of(0)], axis=1, keepdims=True)
    squares = jnp.sum(hidden * hidden, axis=1, keepdims=True)
    wg_in.wait()
    wu_in.wait()
    gate = dot(ag[0], wg[block_of(0), :])
    upper = dot(ag[0], wu[block_of(0), :])
    for k in reversed(order):
        gather_copy(k).wait_recv()
        rows = block_of(nz - k)
        piece = ag[k]
        gate += dot(piece, wg[rows, :])
        upper += dot(piece, wu[rows, :])
        plain = piece.astype(F32) / gf[:, rows]
        squares += jnp.sum(plain * plain, axis=1, keepdims=True)
    scale = lax.rsqrt(squares / model + 1e-6)
    gate = gate * scale
    upper = upper * scale
    middle = (jax.nn.gelu(gate, approximate=True) * upper).astype(BF16).astype(F32)
    tok_score += jnp.sum(middle * w2[...], axis=1, keepdims=True)

    fz[0] = jnp.broadcast_to(jnp.sum(member * tok_score, axis=0, keepdims=True), fz.shape[1:])

    def z_copy(k):
        return pltpu.make_async_remote_copy(
            src_ref=fz.at[0], dst_ref=fz.at[k], send_sem=z_s.at[k], recv_sem=z_r.at[k],
            device_id=((z + k) % nz, p), device_id_type=MESH,
        )

    def p_copy(k):
        return pltpu.make_async_remote_copy(
            src_ref=fp.at[0], dst_ref=fp.at[k], send_sem=p_s.at[k], recv_sem=p_r.at[k],
            device_id=(z, (p + k) % npg), device_id_type=MESH,
        )

    for k in order:
        z_copy(k).start()
    for k in order:
        z_copy(k).wait_recv()
    fp[0] = jnp.sum(fz[...], axis=0)
    for k in range(1, npg):
        p_copy(k).start()
    for k in range(1, npg):
        p_copy(k).wait_recv()
    pooled = jnp.sum(fp[...], axis=0)
    want = iota((doc_dev, fin), 1) == iota((doc_dev, fin), 0) + p * doc_dev
    picked = jnp.sum(jnp.where(want, pooled[0:1, :], 0.0), axis=1, keepdims=True)
    scores = picked / counts
    eye = iota((doc_dev, doc_dev), 0) == iota((doc_dev, doc_dev), 1)
    out[...] = jnp.sum(jnp.where(eye, scores, 0.0), axis=0, keepdims=True)

    for copy in pairs:
        copy.wait_send()
    for k in range(1, nc):
        query_copy(k).wait_send()
        partial_copy(k).wait_send()
    for k in range(1, nz):
        scatter_copy(k).wait_send()
        gather_copy(k).wait_send()
        z_copy(k).wait_send()
    for k in range(1, npg):
        p_copy(k).wait_send()


def per_device(
    nz, npg,
    doc_states, gain_attn, query_weight, cache_keys, cache_values, rel_bucket, bias_table,
    out_weight, gain_ffn, wi_gate, wi_up, wo_ffn, score_vector, query_lengths, doc_query,
    doc_of_token, page_table,
):
    toks, model = doc_states.shape
    width = query_weight.shape[1]
    hidden_units = wi_gate.shape[1]
    heads, buckets = bias_table.shape[1], bias_table.shape[0]
    pages, page_len, _ = cache_keys.shape
    total_toks = doc_of_token.shape[0]
    ndoc = doc_query.shape[0]
    nc = npg // 2
    span = 2 * pages * page_len
    block = model // nz
    fin = max(128, ndoc)
    hbm = pl.BlockSpec(memory_space=pltpu.HBM)
    vmem = pl.BlockSpec(memory_space=pltpu.VMEM)
    dma = pltpu.SemaphoreType.DMA
    result = pl.pallas_call(
        functools.partial(kernel, nz, npg),
        out_shape=jax.ShapeDtypeStruct((1, ndoc // npg), F32),
        in_specs=[hbm] * 17,
        out_specs=vmem,
        scratch_shapes=[
            pltpu.VMEM((1, model), F32),
            pltpu.VMEM((pages, page_len), jnp.int32),
            pltpu.VMEM((heads, buckets), F32),
            pltpu.VMEM((1, model), F32),
            pltpu.VMEM((1, model), F32),
            pltpu.SMEM(query_lengths.shape, jnp.int32),
            pltpu.SMEM(doc_query.shape, jnp.int32),
            pltpu.VMEM((1, total_toks), jnp.int32),
            pltpu.SMEM(page_table.shape, jnp.int32),
            pltpu.VMEM((toks, model), BF16),
            pltpu.VMEM((model, width), BF16),
            pltpu.VMEM((2, pages, page_len, width), BF16),
            pltpu.VMEM((2, pages, page_len, width), BF16),
            pltpu.VMEM((pages, page_len), jnp.int32),
            pltpu.VMEM((width, model), BF16),
            pltpu.VMEM((model, hidden_units), BF16),
            pltpu.VMEM((model, hidden_units), BF16),
            pltpu.VMEM((hidden_units, model), BF16),
            pltpu.VMEM((heads, span, 128), BF16),
            pltpu.VMEM((heads, span, 128), BF16),
            pltpu.VMEM((heads, span), F32),
            pltpu.VMEM((1, total_toks), F32),
            pltpu.VMEM((1, span), F32),
            pltpu.VMEM((nc, toks, width), BF16),
            pltpu.VMEM((nc, toks, width + 128), BF16),
            pltpu.VMEM((nc, toks, width + 128), BF16),
            pltpu.VMEM((nz, toks, block), BF16),
            pltpu.VMEM((nz, toks, block), BF16),
            pltpu.VMEM((nz, toks, block), BF16),
            pltpu.VMEM((nz, 8, fin), F32),
            pltpu.VMEM((npg, 8, fin), F32),
            pltpu.VMEM((1, hidden_units), F32),
            dma((17,)), dma((3,)), dma((3,)),
            dma((nc,)), dma((nc,)), dma((nc,)), dma((nc,)),
            dma((nz,)), dma((nz,)), dma((nz,)), dma((nz,)), dma((nz,)), dma((nz,)),
            dma((npg,)), dma((npg,)),
        ],
        compiler_params=pltpu.CompilerParams(
            collective_id=0, has_side_effects=True, vmem_limit_bytes=56 * 2**20,
        ),
    )(
        doc_states, gain_attn.reshape(1, -1), query_weight, cache_keys, cache_values, rel_bucket,
        bias_table.T, out_weight, gain_ffn.reshape(1, -1), wi_gate, wi_up, wo_ffn,
        score_vector.reshape(1, -1), query_lengths, doc_query, doc_of_token.reshape(1, -1),
        page_table,
    )
    return result.reshape(-1)


def solution(mesh):
    return jax.shard_map(
        functools.partial(per_device, mesh.shape["head"], mesh.shape["page"]),
        mesh=mesh,
        in_specs=(
            P("page", None),
            P(),
            P(None, "head"),
            P("page", None, "head"),
            P("page", None, "head"),
            P("page", None),
            P(None, "head"),
            P("head", None),
            P(),
            P(None, "head"),
            P(None, "head"),
            P("head", None),
            P(),
            P(),
            P(),
            P(),
            P(),
        ),
        out_specs=P("page"),
        check_vma=False,
    )
```

profile of v0, /device:TPU:0, one launch (start us, length us, event | category | flops | bytes accessed | tf_op | source)
XLA Modules:
  0.0 40.3 jit_solution(6234675590908471332)
XLA Ops:
  0.0 39.1 %shard_map.163 = f32[1,8]{1,0:T(1,128)} custom-call(bf16[64,2048]{1,0:T(8,128)(2,1)} %doc_hbm.1, f32[1,2048]{1,0:T(1,128)} %bitcast.6, bf16[2048,512]{1,0:T(8,128)(2,1)} %qw_hbm.1, bf16[2,128,512]{2,1,0:T(8,128)(2,1)} %ck_hbm.1, bf16[2,128,512]{2,1,0:T(8,128)(2,1)} %cv_hbm.1, s32[2,128]{1,0:T(2,128)} %rb_hbm.1, f32[8,32]{1,0:T(8,128)} %bitcast.9, ...), custom_call_target="tpu_custom_call" | custom-call | tf_op jit(solution)/shard_map/pallas_call | solution.py:363
  39.1 1.2 %copy.19 = f32[8]{0:T(128)} copy(f32[8]{0:T(128)} %bitcast.11) | data formatting | bytes 64
where the time goes:
time: 40.4 us; the launch traced here: 40.3 us
  Pallas kernels  39.1 us (97%)
  local copies, waits for them, and re-layouts  1.19 us (3%)
    pallas_call x1, Pallas kernels, per_device(): pl.pallas_call(functools.partial(kernel, nz, npg), out_shape=jax.ShapeDty...  39.1 us
    unnamed x1, local copies, waits for them, and re-layouts  1.19 us

commit v1 on v0

--- a/solution.py
+++ b/solution.py
@@ -20,10 +20,6 @@
 
 def dot(a, b):
     return jnp.dot(a, b, preferred_element_type=F32)
-
-
-def dot_last(a, b):
-    return lax.dot_general(a, b, (((1,), (1,)), ((), ())), preferred_element_type=F32)
 
 
 def three_parts(value):
@@ -40,10 +36,11 @@
     out,
     ga, rb, bt, gf, sv, ql, dq, dtok, pt,
     doc, qw, kbuf, vbuf, rbx, ow, wg, wu, wo, kz, vz, kbias, tokq_row, keyq_row,
-    q_all, ax_out, ax, rs_out, rs, ag, fz, fp, w2,
+    q_all, ax_out, ax, rs_out, rs, ag, fz, fp, svt, w2,
     lsem, pair_s, pair_r, q_s, q_r, a_s, a_r, r_s, r_r, g_s, g_r, z_s, z_r, p_s, p_r,
 ):
     nc = npg // 2
+    group = 3 if (nc - 1) % 3 == 0 else 1
     z = lax.axis_index("head")
     p = lax.axis_index("page")
     core = p % 2
@@ -59,6 +56,7 @@
     ndoc = dq.shape[0]
     doc_dev = ndoc // npg
     block = model // nz
+    part = toks // 2
     all_pages = pt.shape[0]
     max_pages = all_pages // NQ
 
@@ -100,14 +98,19 @@
     qw_in.wait()
     q_all[0] = dot(normed, qw[...]).astype(BF16)
 
-    def query_copy(k):
+    def rows_of(a):
+        return pl.ds(a * part, part)
+
+    def query_copy(k, a):
         return pltpu.make_async_remote_copy(
-            src_ref=q_all.at[0], dst_ref=q_all.at[k], send_sem=q_s.at[k], recv_sem=q_r.at[k],
+            src_ref=q_all.at[0, rows_of(a)], dst_ref=q_all.at[k, rows_of(a)],
+            send_sem=q_s.at[a, k], recv_sem=q_r.at[a, k],
             device_id=(z, ((chip + k) % nc) * 2 + core), device_id_type=MESH,
         )
 
-    for k in range(1, nc):
-        query_copy(k).start()
+    for a in range(2):
+        for k in range(1, nc):
+            query_copy(k, a).start()
     for move in (ow_in, wo_in, wg_in, wu_in):
         move.start()
     for move in small_in:
@@ -139,12 +142,25 @@
     side_mask = [(side == s).astype(F32).astype(BF16) for s in range(128 // depth)]
     per = 128 // depth
 
-    def split_heads(buf, dest, slot):
+    tall = iota((128, 1), 0) // depth
+    tall_mask = [(tall == s).astype(F32) for s in range(per)]
+
+    def split_keys(slot):
         for j in range(pages):
-            rows = pl.ds((slot * pages + j) * page_len, page_len)
+            first = (slot * pages + j) * page_len
+            for g in range(width // 128):
+                flipped = kbuf[slot, j, :, g * 128:(g + 1) * 128].astype(F32).T
+                for s in range(per):
+                    kz[g * per + s, :, first:first + page_len] = (flipped * tall_mask[s]).astype(BF16)
+
+    def split_values(slot):
+        for j in range(pages):
+            first = (slot * pages + j) * page_len
             for h in range(heads):
                 g = h // per
-                dest[h, rows, :] = buf[slot, j, :, g * 128:(g + 1) * 128] * side_mask[h % per]
+                vz[h, first:first + page_len, :] = (
+                    vbuf[slot, j, :, g * 128:(g + 1) * 128] * side_mask[h % per]
+                )
 
     buckets = bt.shape[1]
 
@@ -160,123 +176,165 @@
 
     bias_of(rb, 0)
     k_in.wait()
-    split_heads(kbuf, kz, 0)
+    split_keys(0)
     v_in.wait()
-    split_heads(vbuf, vz, 0)
+    split_values(0)
     for copy in pairs:
         copy.wait_recv()
     bias_of(rbx, 1)
-    split_heads(kbuf, kz, 1)
-    split_heads(vbuf, vz, 1)
+    split_keys(1)
+    split_values(1)
 
     spot = iota((1, 128), 1)
 
-    def token_column(row, first):
-        hit = iota((toks, total_toks), 1) == iota((toks, total_toks), 0) + first
+    def token_column(row, first, count):
+        hit = iota((count, total_toks), 1) == iota((count, total_toks), 0) + first
         return jnp.sum(jnp.where(hit, row, 0.0), axis=1, keepdims=True)
 
-    def attend(k, dest):
-        source = ((chip - k + nc) % nc) * 2 + core
-        column = token_column(tokq_row[...], source * toks)
+    def attend(load, column):
         far = jnp.where(column == keyq_row[...], 0.0, FAR)
-        stats = jnp.zeros((toks, 128), F32)
+        stats = jnp.zeros((column.shape[0], 128), F32)
+        pieces = []
         for base in range(0, heads, 4):
             some = range(base, base + 4)
-            scores = [
-                dot_last(q_all[k, :, h // per * 128:(h // per + 1) * 128], kz[h])
-                + (far + kbias[h:h + 1, :])
-                for h in some
-            ]
+            scores = [dot(load(h // per), kz[h]) + (far + kbias[h:h + 1, :]) for h in some]
             tops = [jnp.max(score, axis=1, keepdims=True) for score in scores]
             weights = [jnp.exp(score - top) for score, top in zip(scores, tops)]
             totals = [jnp.sum(weight, axis=1, keepdims=True) for weight in weights]
             parts = [dot(weight.astype(BF16), vz[h]) for weight, h in zip(weights, some)]
             for h, top, total in zip(some, tops, totals):
-                mine = spot % heads == h
-                stats = jnp.where(mine & (spot < 3 * heads), top, stats)
-                stats = jnp.where(mine & (spot >= 3 * heads), total, stats)
+                own = spot % heads == h
+                stats = jnp.where(own & (spot < 3 * heads), top, stats)
+                stats = jnp.where(own & (spot >= 3 * heads), total, stats)
             for j in range(0, 4, per):
-                g = (base + j) // per
-                dest[:, g * 128:(g + 1) * 128] = sum(parts[j:j + per]).astype(BF16)
-        a, b, c = three_parts(stats)
-        part = (spot // heads) % 3
-        packed = jnp.where(part == 0, a, jnp.where(part == 1, b, c))
-        dest[:, width:] = jnp.where(spot < 6 * heads, packed, 0.0).astype(BF16)
-
-    def partial_copy(k):
+                pieces.append(sum(parts[j:j + per]).astype(BF16))
+        first, second, third = three_parts(stats)
+        turn = (spot // heads) % 3
+        packed = jnp.where(turn == 0, first, jnp.where(turn == 1, second, third))
+        pieces.append(jnp.where(spot < 6 * heads, packed, 0.0).astype(BF16))
+        return pieces
+
+    def partial_copy(k, a):
         return pltpu.make_async_remote_copy(
-            src_ref=ax_out.at[k], dst_ref=ax.at[k], send_sem=a_s.at[k], recv_sem=a_r.at[k],
+            src_ref=ax_out.at[k, rows_of(a)], dst_ref=ax.at[k, rows_of(a)],
+            send_sem=a_s.at[a, k], recv_sem=a_r.at[a, k],
             device_id=(z, ((chip - k + nc) % nc) * 2 + core), device_id_type=MESH,
         )
 
-    attend(0, ax.at[0])
-
-    def serve(k, carry):
-        query_copy(k).wait_recv()
-        attend(k, ax_out.at[k])
-        partial_copy(k).start()
-        return carry
-
-    lax.fori_loop(1, nc, serve, 0)
+    own = attend(
+        lambda g: q_all[0, :, g * 128:(g + 1) * 128], token_column(tokq_row[...], p * toks, toks)
+    )
+    for g, piece in enumerate(own):
+        ax[0, :, g * 128:(g + 1) * 128] = piece
+
+    def serve(a, first):
+        ks = [first + n for n in range(group)]
+        for k in ks:
+            query_copy(k, a).wait_recv()
+        column = jnp.concatenate([
+            token_column(
+                tokq_row[...], (((chip - k + nc) % nc) * 2 + core) * toks + a * part, part
+            )
+            for k in ks
+        ], axis=0)
+
+        def load(g):
+            return jnp.concatenate(
+                [q_all[k, a * part:(a + 1) * part, g * 128:(g + 1) * 128] for k in ks], axis=0
+            )
+
+        for g, piece in enumerate(attend(load, column)):
+            for n, k in enumerate(ks):
+                ax_out[k, a * part:(a + 1) * part, g * 128:(g + 1) * 128] = (
+                    piece[n * part:(n + 1) * part]
+                )
+        for k in ks:
+            partial_copy(k, a).start()
+
+    for a in range(2):
+        if group == nc - 1:
+            serve(a, 1)
+        else:
+            def step(n, carry):
+                serve(a, 1 + n * group)
+                return carry
+
+            lax.fori_loop(0, (nc - 1) // group, step, 0)
+
+    lanes = iota((128, width), 0)
+    same = lanes % heads == iota((128, width), 1) // depth
+    pick_top = (same & (lanes < 3 * heads)).astype(F32).astype(BF16)
+    pick_total = (same & (lanes >= 3 * heads) & (lanes < 6 * heads)).astype(F32).astype(BF16)
+
+    def join(a):
+        rows = slice(a * part, (a + 1) * part)
+        for k in range(1, nc):
+            partial_copy(k, a).wait_recv()
+        tops = [dot(ax[k, rows, width:], pick_top) for k in range(nc)]
+        best = functools.reduce(jnp.maximum, tops)
+        total = jnp.zeros((part, width), F32)
+        sums = jnp.zeros((part, width), F32)
+        for k in range(nc):
+            factor = jnp.exp(tops[k] - best)
+            total += factor * dot(ax[k, rows, width:], pick_total)
+            sums += factor * ax[k, rows, :width].astype(F32)
+        return (sums / total).astype(BF16)
+
+    def block_of(k):
+        return pl.ds(pl.multiple_of(((z + k) % nz) * block, block), block)
+
+    def scatter_copy(k, a):
+        return pltpu.make_async_remote_copy(
+            src_ref=rs_out.at[k, rows_of(a)], dst_ref=rs.at[k, rows_of(a)],
+            send_sem=r_s.at[a, k], recv_sem=r_r.at[a, k],
+            device_id=((z + k) % nz, p), device_id_type=MESH,
+        )
+
+    def gather_copy(k, a):
+        return pltpu.make_async_remote_copy(
+            src_ref=ag.at[0, rows_of(a)], dst_ref=ag.at[k, rows_of(a)],
+            send_sem=g_s.at[a, k], recv_sem=g_r.at[a, k],
+            device_id=((z + k) % nz, p), device_id_type=MESH,
+        )
+
+    order = sorted(range(1, nz), key=lambda k: -min(k, nz - k))
+    ow_in.wait()
+    halves = []
+    for a in range(2):
+        rows = slice(a * part, (a + 1) * part)
+        context = join(a)
+        for k in order:
+            rs_out[k, rows, :] = dot(context, ow[:, block_of(k)]).astype(BF16)
+            scatter_copy(k, a).start()
+        halves.append(doc[rows, block_of(0)].astype(F32) + dot(context, ow[:, block_of(0)]))
 
     wo_in.wait()
-    a, b, c = three_parts(sv[...])
-    line = iota((16, model), 0)
-    folded = jnp.where(line == 0, a, jnp.where(line == 1, b, jnp.where(line == 2, c, 0.0)))
-    w2[...] = jnp.sum(dot_last(folded.astype(BF16), wo[...]), axis=0, keepdims=True)
-    own_docs = token_column(docs.astype(F32), p * toks)
+    first, second, third = three_parts(sv[...])
+    line = iota((128, model), 0)
+    folded = jnp.where(line == 0, first, jnp.where(line == 1, second, jnp.where(line == 2, third, 0.0)))
+    for n in range(model // 128):
+        svt[n * 128:(n + 1) * 128, :] = folded[:, n * 128:(n + 1) * 128].T.astype(BF16)
+    tall_w = jnp.sum(dot(wo[...], svt[...]), axis=1, keepdims=True)
+    first, second, third = three_parts(tall_w)
+    w2[...] = jnp.where(
+        spot == 0, first, jnp.where(spot == 1, second, jnp.where(spot == 2, third, 0.0))
+    ).astype(BF16)
+    own_docs = token_column(docs.astype(F32), p * toks, toks)
     fin = fz.shape[2]
     member = (own_docs == iota((toks, fin), 1).astype(F32)).astype(F32)
     mine = p * doc_dev + iota((doc_dev, total_toks), 0)
     counts = jnp.sum((docs == mine).astype(F32), axis=1, keepdims=True)
-    ow_in.wait()
-
-    lanes = iota((128, width), 0)
-    same = lanes % heads == iota((128, width), 1) // depth
-    pick_top = (same & (lanes < 3 * heads)).astype(F32).astype(BF16)
-    pick_total = (same & (lanes >= 3 * heads) & (lanes < 6 * heads)).astype(F32).astype(BF16)
-    for k in range(1, nc):
-        partial_copy(k).wait_recv()
-    best = dot(ax[0, :, width:], pick_top)
-    for k in range(1, nc):
-        best = jnp.maximum(best, dot(ax[k, :, width:], pick_top))
-    total = jnp.zeros((toks, width), F32)
-    sums = jnp.zeros((toks, width), F32)
-    for k in range(nc):
-        stat = ax[k, :, width:]
-        factor = jnp.exp(dot(stat, pick_top) - best)
-        total += factor * dot(stat, pick_total)
-        sums += factor * ax[k, :, :width].astype(F32)
-    context = (sums / total).astype(BF16)
-
-    def block_of(k):
-        return pl.ds(pl.multiple_of(((z + k) % nz) * block, block), block)
-
-    def scatter_copy(k):
-        return pltpu.make_async_remote_copy(
-            src_ref=rs_out.at[k], dst_ref=rs.at[k], send_sem=r_s.at[k], recv_sem=r_r.at[k],
-            device_id=((z + k) % nz, p), device_id_type=MESH,
-        )
-
-    order = sorted(range(1, nz), key=lambda k: -min(k, nz - k))
-    for k in order:
-        rs_out[k] = dot(context, ow[:, block_of(k)]).astype(BF16)
-        scatter_copy(k).start()
-    hidden = doc[:, block_of(0)].astype(F32) + dot(context, ow[:, block_of(0)])
-    for k in reversed(order):
-        scatter_copy(k).wait_recv()
-        hidden += rs[k].astype(F32)
-
-    def gather_copy(k):
-        return pltpu.make_async_remote_copy(
-            src_ref=ag.at[0], dst_ref=ag.at[k], send_sem=g_s.at[k], recv_sem=g_r.at[k],
-            device_id=((z + k) % nz, p), device_id_type=MESH,
-        )
 
     gain = gf[:, block_of(0)]
-    ag[0] = (hidden * gain).astype(BF16)
-    for k in order:
-        gather_copy(k).start()
+    for a in range(2):
+        rows = slice(a * part, (a + 1) * part)
+        for k in reversed(order):
+            scatter_copy(k, a).wait_recv()
+            halves[a] += rs[k, rows, :].astype(F32)
+        ag[0, rows, :] = (halves[a] * gain).astype(BF16)
+        for k in order:
+            gather_copy(k, a).start()
+    hidden = jnp.concatenate(halves, axis=0)
     tok_score = jnp.sum(hidden * sv[:, block_of(0)], axis=1, keepdims=True)
     squares = jnp.sum(hidden * hidden, axis=1, keepdims=True)
     wg_in.wait()
@@ -284,7 +342,8 @@
     gate = dot(ag[0], wg[block_of(0), :])
     upper = dot(ag[0], wu[block_of(0), :])
     for k in reversed(order):
-        gather_copy(k).wait_recv()
+        gather_copy(k, 0).wait_recv()
+        gather_copy(k, 1).wait_recv()
         rows = block_of(nz - k)
         piece = ag[k]
         gate += dot(piece, wg[rows, :])
@@ -294,8 +353,8 @@
     scale = lax.rsqrt(squares / model + 1e-6)
     gate = gate * scale
     upper = upper * scale
-    middle = (jax.nn.gelu(gate, approximate=True) * upper).astype(BF16).astype(F32)
-    tok_score += jnp.sum(middle * w2[...], axis=1, keepdims=True)
+    middle = (jax.nn.gelu(gate, approximate=True) * upper).astype(BF16)
+    tok_score += jnp.sum(dot(middle, w2[...]), axis=1, keepdims=True)
 
     fz[0] = jnp.broadcast_to(jnp.sum(member * tok_score, axis=0, keepdims=True), fz.shape[1:])
 
@@ -329,12 +388,14 @@
 
     for copy in pairs:
         copy.wait_send()
-    for k in range(1, nc):
-        query_copy(k).wait_send()
-        partial_copy(k).wait_send()
+    for a in range(2):
+        for k in range(1, nc):
+            query_copy(k, a).wait_send()
+            partial_copy(k, a).wait_send()
+        for k in range(1, nz):
+            scatter_copy(k, a).wait_send()
+            gather_copy(k, a).wait_send()
     for k in range(1, nz):
-        scatter_copy(k).wait_send()
-        gather_copy(k).wait_send()
         z_copy(k).wait_send()
     for k in range(1, npg):
         p_copy(k).wait_send()
@@ -384,7 +445,7 @@
             pltpu.VMEM((model, hidden_units), BF16),
             pltpu.VMEM((model, hidden_units), BF16),
             pltpu.VMEM((hidden_units, model), BF16),
-            pltpu.VMEM((heads, span, 128), BF16),
+            pltpu.VMEM((heads, 128, span), BF16),
             pltpu.VMEM((heads, span, 128), BF16),
             pltpu.VMEM((heads, span), F32),
             pltpu.VMEM((1, total_toks), F32),
@@ -397,10 +458,11 @@
             pltpu.VMEM((nz, toks, block), BF16),
             pltpu.VMEM((nz, 8, fin), F32),
             pltpu.VMEM((npg, 8, fin), F32),
-            pltpu.VMEM((1, hidden_units), F32),
+            pltpu.VMEM((model, 128), BF16),
+            pltpu.VMEM((hidden_units, 128), BF16),
             dma((17,)), dma((3,)), dma((3,)),
-            dma((nc,)), dma((nc,)), dma((nc,)), dma((nc,)),
-            dma((nz,)), dma((nz,)), dma((nz,)), dma((nz,)), dma((nz,)), dma((nz,)),
+            dma((2, nc)), dma((2, nc)), dma((2, nc)), dma((2, nc)),
+            dma((2, nz)), dma((2, nz)), dma((2, nz)), dma((2, nz)), dma((nz,)), dma((nz,)),
             dma((npg,)), dma((npg,)),
         ],
         compiler_params=pltpu.CompilerParams(

time: 40.4 us -> 39.4 us (0.975)
  Pallas kernels: 39.1 us -> 38 us
    pallas_call x1, Pallas kernels: 39.1 us -> 38 us  [per_device(): pl.pallas_call(functools.partial(kernel, nz, npg), out_shape=jax.ShapeDty...]
where the time goes in v1:
time: 39.4 us; the launch traced here: 39.2 us
  Pallas kernels  38 us (96%)
  local copies, waits for them, and re-layouts  1.19 us (3%)
    pallas_call x1, Pallas kernels, per_device(): pl.pallas_call(functools.partial(kernel, nz, npg), out_shape=jax.ShapeDty...  38 us
    unnamed x1, local copies, waits for them, and re-layouts  1.19 us

profile of v1, /device:TPU:0, one launch (start us, length us, event | category | flops | bytes accessed | tf_op | source)
XLA Modules:
  0.0 39.2 jit_solution(11620700582307258204)
XLA Ops:
  0.0 38.0 %shard_map.163 = f32[1,8]{1,0:T(1,128)} custom-call(bf16[64,2048]{1,0:T(8,128)(2,1)} %doc_hbm.1, f32[1,2048]{1,0:T(1,128)} %bitcast.6, bf16[2048,512]{1,0:T(8,128)(2,1)} %qw_hbm.1, bf16[2,128,512]{2,1,0:T(8,128)(2,1)} %ck_hbm.1, bf16[2,128,512]{2,1,0:T(8,128)(2,1)} %cv_hbm.1, s32[2,128]{1,0:T(2,128)} %rb_hbm.1, f32[8,32]{1,0:T(8,128)} %bitcast.9, ...), custom_call_target="tpu_custom_call" | custom-call | tf_op jit(solution)/shard_map/pallas_call | solution.py:424
  38.0 1.2 %copy.19 = f32[8]{0:T(128)} copy(f32[8]{0:T(128)} %bitcast.11) | data formatting | bytes 64
